TPU v7x, 32 devices: a whole 2x2x4 slice. The times are simulated.
32 devices in a mesh: dp: 4 (over y, x), expert: 8 (over z, core).
Axes of the slice: x: 2, y: 2, z: 4, core: 2. Of those that a mesh axis runs over, the one named last changes fastest.
Arguments:
- tokens: bfloat16 [8192, 2048], P(('dp', 'expert')), may hold values from -6 to 6
- out_grad: bfloat16 [8192, 2048], P(('dp', 'expert')), may hold values from -6 to 6
- token_picks: int32 [32, 16, 8], P(('dp', 'expert')), may hold values from 0 to 255, as said below
- router: bfloat16 [2048, 16], P(None, 'expert'), may hold values from -0.125 to 0.125
- kept_blocks: int32 [16, 3, 128], P('expert'), may hold values from 0 to 384, as said below
- masters: float32 [16, 3, 128, 4096], P('expert', None, 'dp'), may hold values from -0.25 to 0.25
- scores: float32 [16, 3, 128], P('expert', None, 'dp'), may hold values from -6 to 6
Outputs:
- layer_out: bfloat16 [8192, 2048], P(('dp', 'expert'))
- input_grad: bfloat16 [8192, 2048], P(('dp', 'expert'))
- master_new: float32 [16, 3, 128, 4096], P('expert', None, 'dp')
- score_new: float32 [16, 3, 128], P('expert', None, 'dp')
- router_grad: float32 [2048, 16], P('dp', 'expert')
Inputs may be any that keep to these rules, and one draw needn't show every extreme that they name: `token_picks`: within one source block and one expert the 8 picks are distinct tokens. `kept_blocks`: each list of 128 slots holds, in ascending order, between 64 and 128 distinct block numbers below 384, then 384 in the remaining slots; for each of the three matrices the list of some expert is full.
All inputs are finite; a program needn't handle non-finite values.
Results may differ from a plain program's by a relative error of at most 0.0081.
Values may be sent and summed in bfloat16 or wider, within the bound.
A program may use at most 192 MiB of HBM per device.

v0:
```python
import functools

import jax
import jax.numpy as jnp
from jax import lax
from jax.experimental import pallas as pl
from jax.experimental.pallas import tpu as pltpu
from jax.sharding import PartitionSpec as P

FF = 768
BS = 64
LANES = 2 * BS

LEARN_RATE = 0.005
SCORE_RATE = 0.05

F32 = jnp.float32
BF16 = jnp.bfloat16


def dot(a, b, dims=((1,), (0,))):
    return lax.dot_general(a, b, (dims, ((), ())), preferred_element_type=F32)


def sigma(v):
    return 1.0 / (1.0 + jnp.exp(-v))


def kernel(
    sizes,
    place_ref,
    pick_ref,
    picks_col,
    picks_row,
    tokens,
    out_grad,
    router,
    masters,
    layer_out,
    input_grad,
    master_new,
    score_sum,
    router_out,
    own,
    paired,
    tiles,
    held,
    stage,
    w_gate,
    w_up,
    w_down,
    dense,
    got,
    relay,
    x_send,
    x_got,
    y_got,
    rows,
    scaled,
    hidden,
    pre_gate,
    pre_up,
    outs,
    r_send,
    r_got,
    w_ssem,
    w_rsem,
    g_ssem,
    g_rsem,
    x_ssem,
    x_rsem,
    y_ssem,
    y_rsem,
    r_ssem,
    r_rsem,
):
    n_dp, n_ex, members, cap = sizes
    width = tokens.shape[1]
    in_blocks = width // BS
    hid_blocks = FF // BS
    blocks = in_blocks * hid_blocks
    pairs = masters.shape[1] // 2
    total_pairs = pairs * n_dp
    slots = 2 * total_pairs
    per_peer = members * cap
    all_rows = n_ex * per_peer
    expert_rows = n_ex * cap
    my_dp = lax.axis_index("dp")
    my_ex = lax.axis_index("expert")

    def ahead(i):
        return lax.rem(my_dp + i, n_dp)

    near_a = my_dp + 1 - 2 * (my_dp % 2)
    near_b = my_dp + 2 - 4 * (my_dp // 2)
    across = n_dp - 1 - my_dp

    def peer(i):
        return lax.rem(my_ex + i, n_ex)

    def loop(lo, hi, fn):
        def step(i, carry):
            fn(i)
            return carry

        lax.fori_loop(lo, hi, step, 0)

    barrier = pltpu.get_barrier_semaphore()
    for i in range(1, n_dp):
        pl.semaphore_signal(
            barrier, inc=1, device_id={"dp": ahead(i)}, device_id_type=pl.DeviceIdType.MESH
        )
    loop(
        1,
        n_ex,
        lambda i: pl.semaphore_signal(
            barrier, inc=1, device_id={"expert": peer(i)}, device_id_type=pl.DeviceIdType.MESH
        ),
    )

    chosen = (
        lax.broadcasted_iota(jnp.int32, (all_rows, tokens.shape[0]), 1) == picks_col[...]
    ).astype(F32).astype(BF16)
    x_send[0] = dot(chosen, tokens[...]).astype(BF16).reshape(n_ex, per_peer, width)
    x_send[1] = dot(chosen, out_grad[...]).astype(BF16).reshape(n_ex, per_peer, width)
    stage[2 * total_pairs] = jnp.zeros((BS, LANES), BF16)
    dense[blocks // 2] = jnp.zeros((BS, LANES), F32)

    half_low = lax.broadcasted_iota(jnp.int32, (BS // 2, LANES), 1) < BS
    half = BS // 2

    def pack(c):
        for j in range(half):
            paired[pl.ds(j, 2 * pairs, stride=half), :] = masters[c, :, j * LANES : (j + 1) * LANES]

        def interleave(q):
            first = paired[pl.ds(pl.multiple_of(q * half, half), half), :]
            second = paired[pl.ds(pl.multiple_of((q + pairs) * half, half), half), :]
            tiles[pl.ds(q * BS, half, stride=2), :] = jnp.where(
                half_low, first, pltpu.roll(second, BS, 1)
            )
            tiles[pl.ds(q * BS + 1, half, stride=2), :] = jnp.where(
                half_low, pltpu.roll(first, BS, 1), second
            )

        loop(0, pairs, interleave)

        def narrow(q):
            own[c, q] = tiles[pl.ds(pl.multiple_of(q * BS, BS), BS), :].astype(BF16)

        loop(0, pairs, narrow)

    pack(0)
    pl.semaphore_wait(barrier, n_dp - 1 + n_ex - 1)

    def x_copy(which, i):
        return pltpu.make_async_remote_copy(
            src_ref=x_send.at[which, peer(i)],
            dst_ref=x_got.at[which, my_ex],
            send_sem=x_ssem.at[which, i - 1],
            recv_sem=x_rsem.at[which, i - 1],
            device_id={"expert": peer(i)},
            device_id_type=pl.DeviceIdType.MESH,
        )

    def y_copy(which, i):
        return pltpu.make_async_remote_copy(
            src_ref=x_send.at[which, peer(i)],
            dst_ref=y_got.at[which, my_ex],
            send_sem=y_ssem.at[which, i - 1],
            recv_sem=y_rsem.at[which, i - 1],
            device_id={"expert": peer(i)},
            device_id_type=pl.DeviceIdType.MESH,
        )

    first_half = pl.ds(0, pairs // 2)
    last_half = pl.ds(pairs // 2, pairs // 2)

    def dp_copy(src, dst, send_sem, recv_sem, device):
        return pltpu.make_async_remote_copy(
            src_ref=src,
            dst_ref=dst,
            send_sem=send_sem,
            recv_sem=recv_sem,
            device_id={"dp": device},
            device_id_type=pl.DeviceIdType.MESH,
        )

    def w_copy(c, k):
        src, dst, device = (
            (own.at[c], held.at[c, 0], near_a),
            (own.at[c], held.at[c, 1], near_b),
            (held.at[c, 0, first_half], held.at[c, 2, first_half], near_b),
            (held.at[c, 1, last_half], held.at[c, 2, last_half], near_a),
        )[k]
        return dp_copy(src, dst, w_ssem.at[c, k], w_rsem.at[c, k], device)

    def g_copy(c, k):
        src, dst, device = (
            (held.at[c, 2, first_half], relay.at[c, 0], near_a),
            (held.at[c, 2, last_half], relay.at[c, 1], near_b),
            (held.at[c, 0, first_half], got.at[c, 0, first_half], near_a),
            (held.at[c, 1, last_half], got.at[c, 1, last_half], near_b),
            (held.at[c, 0, last_half], got.at[c, 0, last_half], near_a),
            (held.at[c, 1, first_half], got.at[c, 1, first_half], near_b),
        )[k]
        return dp_copy(src, dst, g_ssem.at[c, k], g_rsem.at[c, k], device)

    def r_copy(i):
        return pltpu.make_async_remote_copy(
            src_ref=r_send,
            dst_ref=r_got.at[i - 1],
            send_sem=r_ssem.at[i - 1],
            recv_sem=r_rsem.at[i - 1],
            device_id={"dp": ahead(i)},
            device_id_type=pl.DeviceIdType.MESH,
        )

    def send_weights(c):
        w_copy(c, 0).start()
        w_copy(c, 1).start()

    def forward(c):
        for k in (0, 1):
            w_copy(c, k).wait_recv()
        for k in (2, 3):
            w_copy(c, k).start()

    send_weights(0)
    loop(1, n_ex, lambda i: x_copy(0, i).start())
    for c in (1, 2):
        pack(c)
        send_weights(c)
    loop(1, n_ex, lambda i: x_copy(1, i).start())
    for which in range(2):
        x_got[which, my_ex] = x_send[which, my_ex]
    loop(3, 3 * members, pack)
    forward(0)
    forward(1)
    send_weights(3)
    forward(2)
    loop(4, 3 * members, send_weights)

    low = lax.broadcasted_iota(jnp.int32, (BS, LANES), 1) < BS

    def load_stage(c):
        def put(base, tile):
            stage[base] = tile
            stage[total_pairs + base] = pltpu.roll(tile.astype(F32), BS, 1).astype(BF16)

        loop(0, pairs, lambda q: put(my_dp * pairs + q, own[c, q]))
        for k, shard in enumerate((near_a, near_b)):
            loop(0, pairs, lambda q: put(shard * pairs + q, held[c, k, q]))
        w_copy(c, 2).wait_recv()
        w_copy(c, 3).wait_recv()
        loop(0, pairs, lambda q: put(across * pairs + q, held[c, 2, q]))

    def assemble(c, target, row_blocks, col_blocks):
        load_stage(c)

        def one_row(r):
            start = pl.multiple_of(r * BS, BS)
            for k in range(col_blocks // 2):
                at = c * blocks + r * col_blocks + 2 * k
                tile = jnp.where(low, stage[place_ref[at]], stage[place_ref[at + 1]])
                target[pl.ds(start, BS), k * LANES : (k + 1) * LANES] = tile

        loop(0, row_blocks, one_row)

    def dense_grad(left, right, row_blocks):
        height = row_blocks * BS
        step = 512 if height % 512 == 0 else height
        for col in range(0, right.shape[1], 2 * LANES):
            for row in range(0, height, step):
                product = dot(
                    left[:, row : row + step], right[:, col : col + 2 * LANES], ((0,), (0,))
                )
                for half in range(2):
                    base = (col // LANES + half) * row_blocks + row // BS
                    dense[base : base + step // BS] = product[
                        :, half * LANES : (half + 1) * LANES
                    ].reshape(step // BS, BS, LANES)

    def extract(c):
        def tile(d, q):
            at = c * slots + d * 2 * pairs + q
            code0 = pick_ref[at]
            code1 = pick_ref[at + pairs]
            first = dense[code0 // 2]
            second = dense[code1 // 2]
            side0 = jnp.full((BS, LANES), code0 % 2, jnp.int32)
            side1 = jnp.full((BS, LANES), code1 % 2, jnp.int32)
            first = jnp.where(side0 == 0, first, pltpu.roll(first, BS, 1))
            second = jnp.where(side1 == 1, second, pltpu.roll(second, BS, 1))
            return jnp.where(low, first, second)

        for k in range(4):
            w_copy(c, k).wait_send()
        for k, shard in ((2, across), (0, near_a), (1, near_b)):

            def fill(q):
                held[c, k, q] = tile(shard, q).astype(BF16)

            loop(0, pairs, fill)
            for g in ((2,), (3,), (0, 1))[k]:
                g_copy(c, g).start()

        def keep(q):
            own[c, q] = tile(my_dp, q).astype(BF16)

        loop(0, pairs, keep)

    def pass_on(c):
        g_copy(c, 0).wait_recv()
        g_copy(c, 1).wait_recv()

        def add(q):
            later = q + pairs // 2
            held[c, 0, later] = (held[c, 0, later].astype(F32) + relay[c, 1, q].astype(F32)).astype(BF16)
            held[c, 1, q] = (held[c, 1, q].astype(F32) + relay[c, 0, q].astype(F32)).astype(BF16)

        loop(0, pairs // 2, add)
        g_copy(c, 4).start()
        g_copy(c, 5).start()

    def order(e):
        at = lax.broadcasted_iota(jnp.int32, (expert_rows, all_rows), 0)
        col = lax.broadcasted_iota(jnp.int32, (expert_rows, all_rows), 1)
        wanted = (at // cap) * per_peer + e * cap + at % cap
        return (col == wanted).astype(F32).astype(BF16)

    def order_back(e):
        col = lax.broadcasted_iota(jnp.int32, (all_rows, expert_rows), 1)
        at = lax.broadcasted_iota(jnp.int32, (all_rows, expert_rows), 0)
        wanted = (col // cap) * per_peer + e * cap + col % cap
        return (at == wanted).astype(F32).astype(BF16)

    def add_part(which, e, part):
        back = dot(order_back(e), part).reshape(n_ex, per_peer, width)
        x_send[which] = (x_send[which].astype(F32) + back).astype(BF16)

    def send_back(which):
        loop(1, n_ex, lambda i: y_copy(which, i).start())
        y_got[which, my_ex] = x_send[which, my_ex]

    def one_expert(e):
        c = 3 * e
        more = e < members - 1
        assemble(c, w_gate, in_blocks, hid_blocks)

        @pl.when(e > 0)
        def _():
            pass_on(c - 2)


        @pl.when(e == 0)
        def _():
            loop(1, n_ex, lambda i: x_copy(0, i).wait_recv())

        rows[...] = dot(order(e), x_got[0].reshape(all_rows, width)).astype(BF16)
        pre_gate[...] = dot(rows[...], w_gate[...])
        gating = sigma(
            jnp.sum(rows[...].astype(F32) * router[e], axis=1, keepdims=True)
        )
        assemble(c + 1, w_up, in_blocks, hid_blocks)
        pl.when(more)(lambda: forward(c + 3))
        pre_up[...] = dot(rows[...], w_up[...])
        gate = pre_gate[...]
        hidden[...] = (gate * sigma(gate) * pre_up[...]).astype(BF16)

        @pl.when(e == 0)
        def _():
            loop(1, n_ex, lambda i: x_copy(1, i).wait_recv())

            def sent(i):
                for which in range(2):
                    x_copy(which, i).wait_send()

            loop(1, n_ex, sent)
            x_send[...] = jnp.zeros(x_send.shape, BF16)

        grad_rows = dot(order(e), x_got[1].reshape(all_rows, width))
        scaled[...] = (gating * grad_rows).astype(BF16)
        dense_grad(hidden, scaled, hid_blocks)
        assemble(c + 2, w_down, hid_blocks, in_blocks)
        extract(c + 2)
        pl.when(more)(lambda: forward(c + 4))
        outs[...] = dot(hidden[...], w_down[...])
        add_part(0, e, (gating * outs[...]).astype(BF16))
        grad_rows = dot(order(e), x_got[1].reshape(all_rows, width))
        logit = (
            jnp.sum(grad_rows * outs[...], axis=1, keepdims=True) * gating * (1.0 - gating)
        )
        r_send[e] = jnp.sum(rows[...].astype(F32) * logit, axis=0, keepdims=True)

        @pl.when(e == members - 1)
        def _():
            for i in range(1, n_dp):
                r_copy(i).start()
            send_back(0)

        pl.when(more)(lambda: forward(c + 5))
        hidden_grad = dot(scaled[...], w_down[...], ((1,), (1,)))
        gate = pre_gate[...]
        sig = sigma(gate)
        gate_grad = hidden_grad * pre_up[...] * sig * (1.0 + gate * (1.0 - sig))
        up_grad = hidden_grad * gate * sig
        pre_gate[...] = gate_grad
        pre_up[...] = up_grad
        dense_grad(rows, pre_gate[...].astype(BF16), in_blocks)
        extract(c)
        pass_on(c + 2)
        dense_grad(rows, pre_up[...].astype(BF16), in_blocks)
        extract(c + 1)
        pass_on(c)
        part = dot(pre_gate[...].astype(BF16), w_gate[...], ((1,), (1,)))
        part = part + dot(pre_up[...].astype(BF16), w_up[...], ((1,), (1,)))
        add_part(1, e, (part + logit * router[e]).astype(BF16))

    loop(0, members, one_expert)
    send_back(1)
    pass_on(3 * members - 2)

    def finish(c):
        for k in range(2, 6):
            g_copy(c, k).wait_recv()

        def add(q):
            total = own[c, q].astype(F32)
            for k in range(2):
                total = total + got[c, k, q].astype(F32)
            tiles[pl.ds(pl.multiple_of(q * BS, BS), BS), :] = total

        loop(0, pairs, add)

        def separate(q):
            even = tiles[pl.ds(q * BS, half, stride=2), :]
            odd = tiles[pl.ds(q * BS + 1, half, stride=2), :]
            paired[pl.ds(pl.multiple_of(q * half, half), half), :] = jnp.where(
                half_low, even, pltpu.roll(odd, BS, 1)
            )
            paired[pl.ds(pl.multiple_of((q + pairs) * half, half), half), :] = jnp.where(
                half_low, pltpu.roll(even, BS, 1), odd
            )

        loop(0, pairs, separate)
        score = jnp.zeros((2 * pairs, LANES), F32)
        for j in range(half):
            part = paired[pl.ds(j, 2 * pairs, stride=half), :]
            master = masters[c, :, j * LANES : (j + 1) * LANES]
            master_new[c, :, j * LANES : (j + 1) * LANES] = master - LEARN_RATE * part
            score = score + master * part
        score_sum[c] = jnp.sum(score, axis=1, keepdims=True)

    def finish_expert(e):
        for m in (2, 0, 1):
            finish(3 * e + m)

    loop(0, members - 1, finish_expert)
    placed = (
        lax.broadcasted_iota(jnp.int32, (tokens.shape[0], all_rows), 0) == picks_row[...]
    ).astype(F32).astype(BF16)
    loop(1, n_ex, lambda i: y_copy(0, i).wait_recv())
    layer_out[...] = dot(placed, y_got[0].reshape(all_rows, width)).astype(BF16)
    loop(1, n_ex, lambda i: y_copy(1, i).wait_recv())
    input_grad[...] = dot(placed, y_got[1].reshape(all_rows, width)).astype(BF16)

    for i in range(1, n_dp):
        r_copy(i).wait()
    share = width // n_dp
    mine = pl.ds(pl.multiple_of(my_dp * share, share), share)
    for e in range(members):
        router_total = r_send[e, :, mine]
        for i in range(1, n_dp):
            router_total = router_total + r_got[i - 1, e, :, mine]
        router_out[e] = router_total

    finish_expert(members - 1)

    def drain_weights(c):
        for k in range(6):
            g_copy(c, k).wait_send()

    loop(0, 3 * members, drain_weights)

    def drain_rows(i):
        for which in range(2):
            y_copy(which, i).wait_send()

    loop(1, n_ex, drain_rows)


def body(tokens, out_grad, token_picks, router, kept_blocks, masters, scores):
    members = kept_blocks.shape[0]
    slots = kept_blocks.shape[2]
    n_ex = lax.axis_size("expert")
    n_dp = lax.axis_size("dp")
    cap = token_picks.shape[2]
    width = tokens.shape[1]
    in_blocks = width // BS
    hid_blocks = FF // BS
    blocks = in_blocks * hid_blocks
    local = masters.shape[2]
    pairs = local // 2
    total_pairs = pairs * n_dp
    chunks = 3 * members
    all_rows = n_ex * members * cap
    expert_rows = n_ex * cap

    kept = kept_blocks.reshape(chunks, slots)
    numbers = jnp.arange(blocks, dtype=jnp.int32)
    hits = kept[:, None, :] == numbers[None, :, None]
    slot_of = jnp.sum(
        jnp.where(hits, jnp.arange(slots, dtype=jnp.int32) + 1, 0), axis=2
    ) - 1
    within = slot_of % local
    flipped = (within // pairs) != (numbers % 2)[None, :]
    place = (slot_of // local) * pairs + within % pairs + jnp.where(flipped, total_pairs, 0)
    place = jnp.where(slot_of >= 0, place, 2 * total_pairs).reshape(-1)

    col_counts = jnp.array([hid_blocks, hid_blocks, in_blocks] * members, jnp.int32)[:, None]
    row_counts = jnp.array([in_blocks, in_blocks, hid_blocks] * members, jnp.int32)[:, None]
    block_row = kept // col_counts
    block_col = kept % col_counts
    code = ((block_col // 2) * row_counts + block_row) * 2 + block_col % 2
    code = jnp.where(kept < blocks, code, blocks).reshape(-1)

    picks = token_picks[0].reshape(-1)
    router_rows = router.T.astype(F32).reshape(members, 1, width)

    vmem = pl.BlockSpec(memory_space=pltpu.VMEM)
    smem = pl.BlockSpec(memory_space=pltpu.SMEM)
    dma = pltpu.SemaphoreType.DMA
    layer_out, input_grad, master_new, score_sum, router_grad = pl.pallas_call(
        functools.partial(kernel, (n_dp, n_ex, members, cap)),
        out_shape=(
            jax.ShapeDtypeStruct(tokens.shape, BF16),
            jax.ShapeDtypeStruct(tokens.shape, BF16),
            jax.ShapeDtypeStruct((chunks, local, BS * BS), F32),
            jax.ShapeDtypeStruct((chunks, local, 1), F32),
            jax.ShapeDtypeStruct((members, 1, width // n_dp), F32),
        ),
        in_specs=[smem, smem] + [vmem] * 6,
        out_specs=[vmem] * 5,
        scratch_shapes=[
            pltpu.VMEM((chunks, pairs, BS, LANES), BF16),
            pltpu.VMEM((local * BS // 2, LANES), F32),
            pltpu.VMEM((pairs * BS, LANES), F32),
            pltpu.VMEM((chunks, n_dp - 1, pairs, BS, LANES), BF16),
            pltpu.VMEM((2 * total_pairs + 1, BS, LANES), BF16),
            pltpu.VMEM((width, FF), BF16),
            pltpu.VMEM((width, FF), BF16),
            pltpu.VMEM((FF, width), BF16),
            pltpu.VMEM((blocks // 2 + 1, BS, LANES), F32),
            pltpu.VMEM((chunks, 2, pairs, BS, LANES), BF16),
            pltpu.VMEM((chunks, 2, pairs // 2, BS, LANES), BF16),
            pltpu.VMEM((2, n_ex, members * cap, width), BF16),
            pltpu.VMEM((2, n_ex, members * cap, width), BF16),
            pltpu.VMEM((2, n_ex, members * cap, width), BF16),
            pltpu.VMEM((expert_rows, width), BF16),
            pltpu.VMEM((expert_rows, width), BF16),
            pltpu.VMEM((expert_rows, FF), BF16),
            pltpu.VMEM((expert_rows, FF), F32),
            pltpu.VMEM((expert_rows, FF), F32),
            pltpu.VMEM((expert_rows, width), F32),
            pltpu.VMEM((members, 1, width), F32),
            pltpu.VMEM((n_dp - 1, members, 1, width), F32),
            dma((chunks, 4)),
            dma((chunks, 4)),
            dma((chunks, 6)),
            dma((chunks, 6)),
            dma((2, n_ex - 1)),
            dma((2, n_ex - 1)),
            dma((2, n_ex - 1)),
            dma((2, n_ex - 1)),
            dma((n_dp - 1,)),
            dma((n_dp - 1,)),
        ],
        compiler_params=pltpu.CompilerParams(
            collective_id=0, has_side_effects=True, vmem_limit_bytes=62 * 1024 * 1024
        ),
    )(
        place,
        code,
        picks.reshape(all_rows, 1),
        picks.reshape(1, all_rows),
        tokens,
        out_grad,
        router_rows,
        masters.reshape(chunks, local, BS * BS),
    )

    master_new = master_new.reshape(masters.shape)
    score_new = scores - SCORE_RATE * score_sum.reshape(scores.shape)
    return layer_out, input_grad, master_new, score_new, router_grad.reshape(members, -1).T


def solution(mesh):
    return jax.shard_map(
        body,
        mesh=mesh,
        in_specs=(
            P(("dp", "expert"), None),
            P(("dp", "expert"), None),
            P(("dp", "expert"), None, None),
            P(None, "expert"),
            P("expert", None, None),
            P("expert", None, "dp", None),
            P("expert", None, "dp"),
        ),
        out_specs=(
            P(("dp", "expert"), None),
            P(("dp", "expert"), None),
            P("expert", None, "dp", None),
            P("expert", None, "dp"),
            P("dp", "expert"),
        ),
        check_vma=False,
    )
```

profile of v0, /device:TPU:0, one launch (start us, length us, event | category | flops | bytes accessed | tf_op | source)
XLA Modules:
  0.0 151.7 jit_solution(9573463804399931725)
XLA Ops:
  0.7 0.7 copy.25
  1.4 1.5 fusion.14.pick_ref
  2.8 0.4 select_reduce_fusion
  3.2 0.8 copy.27
  4.0 0.6 reshape_reshape_squeeze.7.picks_row
  4.6 0.6 fusion.3.place_ref
  5.2 0.7 convert_bitcast_fusion
  5.9 0.6 reshape.70.router
  6.6 0.7 reshape_reshape_squeeze.8.picks_col
  7.3 0.0 copy-start.2
  7.3 136.3 %shard_map.128 = (bf16[256,2048]{1,0:T(8,128)(2,1)}, bf16[256,2048]{1,0:T(8,128)(2,1)}, f32[6,32,4096]{2,1,0:T(8,128)}, f32[6,32,1]{2,1,0:T(8,128)}, f32[2,1,512]{2,1,0:T(1,128)}) custom-call(s32[2304]{0:T(1024)} %fusion.3.place_ref, s32[768]{0:T(1024)} %fusion.14.pick_ref, s32[128,1]{1,0:T(8,128)} %reshape_reshape_squeeze.8.picks_col, ...), custom_call_target="tpu_custom_call" | custom-call | tf_op jit(solution)/shard_map/pallas_call | solution.py:534
  143.6 0.0 copy-start.1
  143.6 1.1 multiply_reduce_fusion
  144.7 0.0 copy-done.2
  144.7 0.6 copy.31
  145.3 1.3 copy.35
  146.6 0.0 copy-start
  146.6 2.5 %copy.39 = bf16[256,2048]{1,0:T(8,128)(2,1)} copy(bf16[256,2048]{1,0:T(8,128)(2,1)} %get-tuple-element.30) | data formatting | bytes 2097152
  149.0 0.0 copy-done.1
  149.0 1.0 copy.40
  150.0 0.0 copy-done
  150.0 1.7 %copy.41 = f32[2,3,32,4096]{3,2,1,0:T(8,128)} copy(f32[2,3,32,4096]{3,2,1,0:T(8,128)S(1)} %bitcast.27) | data formatting | bytes 6291456
  (10 shorter events, 0.1 us)
Async XLA Ops:
  7.3 137.4 %copy-start.2 = (f32[2,3,32]{2,0,1:T(2,128)S(1)}, f32[2,3,32]{2,0,1:T(2,128)}, u32[]{:S(2)}) copy-start(f32[2,3,32]{2,0,1:T(2,128)} %param.15) | copy-start | bytes 2308
  143.6 5.4 %copy-start.1 = (bf16[256,2048]{1,0:T(8,128)(2,1)S(1)}, bf16[256,2048]{1,0:T(8,128)(2,1)}, u32[]{:S(2)}) copy-start(bf16[256,2048]{1,0:T(8,128)(2,1)} %get-tuple-element.31) | copy-start | bytes 3145732
  146.6 3.4 %copy-start = (f32[6,32,4096]{2,1,0:T(8,128)S(1)}, f32[6,32,4096]{2,1,0:T(8,128)}, u32[]{:S(2)}) copy-start(f32[6,32,4096]{2,1,0:T(8,128)} %get-tuple-element.12) | copy-start | bytes 9437188
where the time goes:
time: 153 us; the launch traced here: 152 us
  Pallas kernels  136 us (89%)
  local copies, waits for them, and re-layouts  10.4 us (7%)
  other arithmetic  4.27 us (3%)
    pallas_call x1, Pallas kernels, body(): pl.pallas_call(functools.partial(kernel, (n_dp, n_ex, members, cap)), out...  136 us
    unnamed x13, local copies, waits for them, and re-layouts  8.39 us

commit v1 on v0

--- a/solution.py
+++ b/solution.py
@@ -49,7 +49,10 @@
     w_gate,
     w_up,
     w_down,
-    dense,
+    rows_t,
+    hidden_t,
+    scaled_t,
+    inner_t,
     got,
     relay,
     x_send,
@@ -98,12 +101,12 @@
     def peer(i):
         return lax.rem(my_ex + i, n_ex)
 
-    def loop(lo, hi, fn):
+    def loop(lo, hi, fn, unroll=1):
         def step(i, carry):
             fn(i)
             return carry
 
-        lax.fori_loop(lo, hi, step, 0)
+        lax.fori_loop(lo, hi, step, 0, unroll=unroll)
 
     barrier = pltpu.get_barrier_semaphore()
     for i in range(1, n_dp):
@@ -124,7 +127,16 @@
     x_send[0] = dot(chosen, tokens[...]).astype(BF16).reshape(n_ex, per_peer, width)
     x_send[1] = dot(chosen, out_grad[...]).astype(BF16).reshape(n_ex, per_peer, width)
     stage[2 * total_pairs] = jnp.zeros((BS, LANES), BF16)
-    dense[blocks // 2] = jnp.zeros((BS, LANES), F32)
+    rows_t[in_blocks] = jnp.zeros((BS, expert_rows), BF16)
+    hidden_t[hid_blocks] = jnp.zeros((BS, expert_rows), BF16)
+    same = (
+        lax.broadcasted_iota(jnp.int32, (expert_rows, expert_rows), 0)
+        == lax.broadcasted_iota(jnp.int32, (expert_rows, expert_rows), 1)
+    ).astype(F32).astype(BF16)
+
+    def turned(value):
+        return dot(value, same, ((0,), (0,))).astype(BF16).reshape(-1, BS, expert_rows)
+
 
     half_low = lax.broadcasted_iota(jnp.int32, (BS // 2, LANES), 1) < BS
     half = BS // 2
@@ -143,12 +155,12 @@
                 half_low, pltpu.roll(first, BS, 1), second
             )
 
-        loop(0, pairs, interleave)
+        loop(0, pairs, interleave, 4)
 
         def narrow(q):
             own[c, q] = tiles[pl.ds(pl.multiple_of(q * BS, BS), BS), :].astype(BF16)
 
-        loop(0, pairs, narrow)
+        loop(0, pairs, narrow, 4)
 
     pack(0)
     pl.semaphore_wait(barrier, n_dp - 1 + n_ex - 1)
@@ -248,12 +260,12 @@
             stage[base] = tile
             stage[total_pairs + base] = pltpu.roll(tile.astype(F32), BS, 1).astype(BF16)
 
-        loop(0, pairs, lambda q: put(my_dp * pairs + q, own[c, q]))
+        loop(0, pairs, lambda q: put(my_dp * pairs + q, own[c, q]), 4)
         for k, shard in enumerate((near_a, near_b)):
-            loop(0, pairs, lambda q: put(shard * pairs + q, held[c, k, q]))
+            loop(0, pairs, lambda q: put(shard * pairs + q, held[c, k, q]), 4)
         w_copy(c, 2).wait_recv()
         w_copy(c, 3).wait_recv()
-        loop(0, pairs, lambda q: put(across * pairs + q, held[c, 2, q]))
+        loop(0, pairs, lambda q: put(across * pairs + q, held[c, 2, q]), 4)
 
     def assemble(c, target, row_blocks, col_blocks):
         load_stage(c)
@@ -265,34 +277,23 @@
                 tile = jnp.where(low, stage[place_ref[at]], stage[place_ref[at + 1]])
                 target[pl.ds(start, BS), k * LANES : (k + 1) * LANES] = tile
 
-        loop(0, row_blocks, one_row)
-
-    def dense_grad(left, right, row_blocks):
-        height = row_blocks * BS
-        step = 512 if height % 512 == 0 else height
-        for col in range(0, right.shape[1], 2 * LANES):
-            for row in range(0, height, step):
-                product = dot(
-                    left[:, row : row + step], right[:, col : col + 2 * LANES], ((0,), (0,))
-                )
-                for half in range(2):
-                    base = (col // LANES + half) * row_blocks + row // BS
-                    dense[base : base + step // BS] = product[
-                        :, half * LANES : (half + 1) * LANES
-                    ].reshape(step // BS, BS, LANES)
-
-    def extract(c):
+        loop(0, row_blocks, one_row, 2)
+
+    def extract(c, left, right):
+        def slot(at):
+            code = pick_ref[at]
+            return left[code // BS], right[code % BS]
+
         def tile(d, q):
             at = c * slots + d * 2 * pairs + q
-            code0 = pick_ref[at]
-            code1 = pick_ref[at + pairs]
-            first = dense[code0 // 2]
-            second = dense[code1 // 2]
-            side0 = jnp.full((BS, LANES), code0 % 2, jnp.int32)
-            side1 = jnp.full((BS, LANES), code1 % 2, jnp.int32)
-            first = jnp.where(side0 == 0, first, pltpu.roll(first, BS, 1))
-            second = jnp.where(side1 == 1, second, pltpu.roll(second, BS, 1))
-            return jnp.where(low, first, second)
+            left0, right0 = slot(at)
+            left1, right1 = slot(at + pairs)
+            both = dot(
+                jnp.concatenate([left0, left1], axis=0),
+                jnp.concatenate([right0, right1], axis=0),
+                ((1,), (1,)),
+            )
+            return jnp.where(low, both[:BS], both[BS:])
 
         for k in range(4):
             w_copy(c, k).wait_send()
@@ -301,14 +302,14 @@
             def fill(q):
                 held[c, k, q] = tile(shard, q).astype(BF16)
 
-            loop(0, pairs, fill)
+            loop(0, pairs, fill, 4)
             for g in ((2,), (3,), (0, 1))[k]:
                 g_copy(c, g).start()
 
         def keep(q):
             own[c, q] = tile(my_dp, q).astype(BF16)
 
-        loop(0, pairs, keep)
+        loop(0, pairs, keep, 4)
 
     def pass_on(c):
         g_copy(c, 0).wait_recv()
@@ -319,7 +320,7 @@
             held[c, 0, later] = (held[c, 0, later].astype(F32) + relay[c, 1, q].astype(F32)).astype(BF16)
             held[c, 1, q] = (held[c, 1, q].astype(F32) + relay[c, 0, q].astype(F32)).astype(BF16)
 
-        loop(0, pairs // 2, add)
+        loop(0, pairs // 2, add, 4)
         g_copy(c, 4).start()
         g_copy(c, 5).start()
 
@@ -358,6 +359,7 @@
             loop(1, n_ex, lambda i: x_copy(0, i).wait_recv())
 
         rows[...] = dot(order(e), x_got[0].reshape(all_rows, width)).astype(BF16)
+        rows_t[pl.ds(0, in_blocks)] = turned(rows[...])
         pre_gate[...] = dot(rows[...], w_gate[...])
         gating = sigma(
             jnp.sum(rows[...].astype(F32) * router[e], axis=1, keepdims=True)
@@ -381,9 +383,10 @@
 
         grad_rows = dot(order(e), x_got[1].reshape(all_rows, width))
         scaled[...] = (gating * grad_rows).astype(BF16)
-        dense_grad(hidden, scaled, hid_blocks)
+        hidden_t[pl.ds(0, hid_blocks)] = turned(hidden[...])
+        scaled_t[...] = turned(scaled[...])
         assemble(c + 2, w_down, hid_blocks, in_blocks)
-        extract(c + 2)
+        extract(c + 2, hidden_t, scaled_t)
         pl.when(more)(lambda: forward(c + 4))
         outs[...] = dot(hidden[...], w_down[...])
         add_part(0, e, (gating * outs[...]).astype(BF16))
@@ -407,11 +410,11 @@
         up_grad = hidden_grad * gate * sig
         pre_gate[...] = gate_grad
         pre_up[...] = up_grad
-        dense_grad(rows, pre_gate[...].astype(BF16), in_blocks)
-        extract(c)
+        inner_t[...] = turned(pre_gate[...].astype(BF16))
+        extract(c, rows_t, inner_t)
         pass_on(c + 2)
-        dense_grad(rows, pre_up[...].astype(BF16), in_blocks)
-        extract(c + 1)
+        inner_t[...] = turned(pre_up[...].astype(BF16))
+        extract(c + 1, rows_t, inner_t)
         pass_on(c)
         part = dot(pre_gate[...].astype(BF16), w_gate[...], ((1,), (1,)))
         part = part + dot(pre_up[...].astype(BF16), w_up[...], ((1,), (1,)))
@@ -431,7 +434,7 @@
                 total = total + got[c, k, q].astype(F32)
             tiles[pl.ds(pl.multiple_of(q * BS, BS), BS), :] = total
 
-        loop(0, pairs, add)
+        loop(0, pairs, add, 4)
 
         def separate(q):
             even = tiles[pl.ds(q * BS, half, stride=2), :]
@@ -443,7 +446,7 @@
                 half_low, pltpu.roll(even, BS, 1), odd
             )
 
-        loop(0, pairs, separate)
+        loop(0, pairs, separate, 4)
         score = jnp.zeros((2 * pairs, LANES), F32)
         for j in range(half):
             part = paired[pl.ds(j, 2 * pairs, stride=half), :]
@@ -519,11 +522,9 @@
     place = jnp.where(slot_of >= 0, place, 2 * total_pairs).reshape(-1)
 
     col_counts = jnp.array([hid_blocks, hid_blocks, in_blocks] * members, jnp.int32)[:, None]
-    row_counts = jnp.array([in_blocks, in_blocks, hid_blocks] * members, jnp.int32)[:, None]
-    block_row = kept // col_counts
-    block_col = kept % col_counts
-    code = ((block_col // 2) * row_counts + block_row) * 2 + block_col % 2
-    code = jnp.where(kept < blocks, code, blocks).reshape(-1)
+    empty = jnp.array([in_blocks, in_blocks, hid_blocks] * members, jnp.int32)[:, None] * BS
+    code = (kept // col_counts) * BS + kept % col_counts
+    code = jnp.where(kept < blocks, code, empty).reshape(-1)
 
     picks = token_picks[0].reshape(-1)
     router_rows = router.T.astype(F32).reshape(members, 1, width)
@@ -551,7 +552,10 @@
             pltpu.VMEM((width, FF), BF16),
             pltpu.VMEM((width, FF), BF16),
             pltpu.VMEM((FF, width), BF16),
-            pltpu.VMEM((blocks // 2 + 1, BS, LANES), F32),
+            pltpu.VMEM((in_blocks + 1, BS, expert_rows), BF16),
+            pltpu.VMEM((hid_blocks + 1, BS, expert_rows), BF16),
+            pltpu.VMEM((in_blocks, BS, expert_rows), BF16),
+            pltpu.VMEM((hid_blocks, BS, expert_rows), BF16),
             pltpu.VMEM((chunks, 2, pairs, BS, LANES), BF16),
             pltpu.VMEM((chunks, 2, pairs // 2, BS, LANES), BF16),
             pltpu.VMEM((2, n_ex, members * cap, width), BF16),

time: 153 us -> 135 us (0.88)
  Pallas kernels: 136 us -> 119 us
    pallas_call x1, Pallas kernels: 136 us -> 119 us  [body(): pl.pallas_call(functools.partial(kernel, (n_dp, n_ex, members, cap)), out...]
where the time goes in v1:
time: 135 us; the launch traced here: 134 us
  Pallas kernels  119 us (88%)
  local copies, waits for them, and re-layouts  10.4 us (8%)
  other arithmetic  4.26 us (3%)
    pallas_call x1, Pallas kernels, body(): pl.pallas_call(functools.partial(kernel, (n_dp, n_ex, members, cap)), out...  119 us
    unnamed x13, local copies, waits for them, and re-layouts  8.39 us

profile of v1, /device:TPU:0, one launch (start us, length us, event | category | flops | bytes accessed | tf_op | source)
XLA Modules:
  0.0 134.5 jit_solution(5331583884798964134)
XLA Ops:
  0.7 0.7 copy.25
  1.4 1.5 %fusion.12.pick_ref = s32[768]{0:T(1024)} fusion(s32[768]{0:T(1024)S(1)} %reshape.64, s32[6]{0:T(128)} %constant.104, s32[6]{0:T(128)} %constant.93.clone), kind=kLoop, calls=%fused_computation.33 | loop fusion | flops 12288 | bytes 6192 | tf_op jit(solution)/shard_map/jit(_where)/select_n | solution.py:527
  2.8 0.4 select_reduce_fusion
  3.2 0.8 copy.27
  4.0 0.6 reshape_reshape_squeeze.7.picks_row
  4.6 0.6 fusion.3.place_ref
  5.2 0.7 convert_bitcast_fusion
  5.9 0.6 reshape.71.router
  6.5 0.7 reshape_reshape_squeeze.8.picks_col
  7.3 0.0 copy-start.2
  7.3 119.1 %shard_map.128 = (bf16[256,2048]{1,0:T(8,128)(2,1)}, bf16[256,2048]{1,0:T(8,128)(2,1)}, f32[6,32,4096]{2,1,0:T(8,128)}, f32[6,32,1]{2,1,0:T(8,128)}, f32[2,1,512]{2,1,0:T(1,128)}) custom-call(s32[2304]{0:T(1024)} %fusion.3.place_ref, s32[768]{0:T(1024)} %fusion.12.pick_ref, s32[128,1]{1,0:T(8,128)} %reshape_reshape_squeeze.8.picks_col, ...), custom_call_target="tpu_custom_call" | custom-call | tf_op jit(solution)/shard_map/pallas_call | solution.py:535
  126.4 0.0 copy-start.1
  126.4 1.1 multiply_reduce_fusion
  127.5 0.0 copy-done.2
  127.5 0.6 copy.31
  128.1 1.3 copy.35
  129.4 0.0 copy-start
  129.4 2.5 %copy.39 = bf16[256,2048]{1,0:T(8,128)(2,1)} copy(bf16[256,2048]{1,0:T(8,128)(2,1)} %get-tuple-element.30) | data formatting | bytes 2097152
  131.8 0.0 copy-done.1
  131.8 1.0 copy.40
  132.8 0.0 copy-done
  132.8 1.7 %copy.41 = f32[2,3,32,4096]{3,2,1,0:T(8,128)} copy(f32[2,3,32,4096]{3,2,1,0:T(8,128)S(1)} %bitcast.27) | data formatting | bytes 6291456
  (10 shorter events, 0.1 us)
Async XLA Ops:
  7.3 120.2 %copy-start.2 = (f32[2,3,32]{2,0,1:T(2,128)S(1)}, f32[2,3,32]{2,0,1:T(2,128)}, u32[]{:S(2)}) copy-start(f32[2,3,32]{2,0,1:T(2,128)} %param.15) | copy-start | bytes 2308
  126.4 5.4 %copy-start.1 = (bf16[256,2048]{1,0:T(8,128)(2,1)S(1)}, bf16[256,2048]{1,0:T(8,128)(2,1)}, u32[]{:S(2)}) copy-start(bf16[256,2048]{1,0:T(8,128)(2,1)} %get-tuple-element.31) | copy-start | bytes 3145732
  129.4 3.4 %copy-start = (f32[6,32,4096]{2,1,0:T(8,128)S(1)}, f32[6,32,4096]{2,1,0:T(8,128)}, u32[]{:S(2)}) copy-start(f32[6,32,4096]{2,1,0:T(8,128)} %get-tuple-element.12) | copy-start | bytes 9437188

commit v2 on v1

--- a/solution.py
+++ b/solution.py
@@ -155,12 +155,12 @@
                 half_low, pltpu.roll(first, BS, 1), second
             )
 
-        loop(0, pairs, interleave, 4)
+        loop(0, pairs, interleave, 8)
 
         def narrow(q):
             own[c, q] = tiles[pl.ds(pl.multiple_of(q * BS, BS), BS), :].astype(BF16)
 
-        loop(0, pairs, narrow, 4)
+        loop(0, pairs, narrow, 8)
 
     pack(0)
     pl.semaphore_wait(barrier, n_dp - 1 + n_ex - 1)
@@ -240,18 +240,15 @@
 
     send_weights(0)
     loop(1, n_ex, lambda i: x_copy(0, i).start())
-    for c in (1, 2):
-        pack(c)
-        send_weights(c)
+    pack(1)
+    send_weights(1)
     loop(1, n_ex, lambda i: x_copy(1, i).start())
     for which in range(2):
         x_got[which, my_ex] = x_send[which, my_ex]
-    loop(3, 3 * members, pack)
+    loop(2, 3 * members, pack)
     forward(0)
     forward(1)
-    send_weights(3)
-    forward(2)
-    loop(4, 3 * members, send_weights)
+    send_weights(2)
 
     low = lax.broadcasted_iota(jnp.int32, (BS, LANES), 1) < BS
 
@@ -260,12 +257,12 @@
             stage[base] = tile
             stage[total_pairs + base] = pltpu.roll(tile.astype(F32), BS, 1).astype(BF16)
 
-        loop(0, pairs, lambda q: put(my_dp * pairs + q, own[c, q]), 4)
+        loop(0, pairs, lambda q: put(my_dp * pairs + q, own[c, q]), 8)
         for k, shard in enumerate((near_a, near_b)):
-            loop(0, pairs, lambda q: put(shard * pairs + q, held[c, k, q]), 4)
+            loop(0, pairs, lambda q: put(shard * pairs + q, held[c, k, q]), 8)
         w_copy(c, 2).wait_recv()
         w_copy(c, 3).wait_recv()
-        loop(0, pairs, lambda q: put(across * pairs + q, held[c, 2, q]), 4)
+        loop(0, pairs, lambda q: put(across * pairs + q, held[c, 2, q]), 8)
 
     def assemble(c, target, row_blocks, col_blocks):
         load_stage(c)
@@ -277,7 +274,7 @@
                 tile = jnp.where(low, stage[place_ref[at]], stage[place_ref[at + 1]])
                 target[pl.ds(start, BS), k * LANES : (k + 1) * LANES] = tile
 
-        loop(0, row_blocks, one_row, 2)
+        loop(0, row_blocks, one_row, 4)
 
     def extract(c, left, right):
         def slot(at):
@@ -302,14 +299,14 @@
             def fill(q):
                 held[c, k, q] = tile(shard, q).astype(BF16)
 
-            loop(0, pairs, fill, 4)
+            loop(0, pairs, fill, 8)
             for g in ((2,), (3,), (0, 1))[k]:
                 g_copy(c, g).start()
 
         def keep(q):
             own[c, q] = tile(my_dp, q).astype(BF16)
 
-        loop(0, pairs, keep, 4)
+        loop(0, pairs, keep, 8)
 
     def pass_on(c):
         g_copy(c, 0).wait_recv()
@@ -347,25 +344,29 @@
     def one_expert(e):
         c = 3 * e
         more = e < members - 1
+
+        @pl.when(e == 0)
+        def _():
+            loop(1, n_ex, lambda i: x_copy(0, i).wait_recv())
+
+        rows[...] = dot(order(e), x_got[0].reshape(all_rows, width)).astype(BF16)
+        rows_t[pl.ds(0, in_blocks)] = turned(rows[...])
+        gating = sigma(
+            jnp.sum(rows[...].astype(F32) * router[e], axis=1, keepdims=True)
+        )
         assemble(c, w_gate, in_blocks, hid_blocks)
+
+        @pl.when(e == 0)
+        def _():
+            forward(2)
+            loop(3, 3 * members, send_weights)
 
         @pl.when(e > 0)
         def _():
             pass_on(c - 2)
 
-
-        @pl.when(e == 0)
-        def _():
-            loop(1, n_ex, lambda i: x_copy(0, i).wait_recv())
-
-        rows[...] = dot(order(e), x_got[0].reshape(all_rows, width)).astype(BF16)
-        rows_t[pl.ds(0, in_blocks)] = turned(rows[...])
         pre_gate[...] = dot(rows[...], w_gate[...])
-        gating = sigma(
-            jnp.sum(rows[...].astype(F32) * router[e], axis=1, keepdims=True)
-        )
         assemble(c + 1, w_up, in_blocks, hid_blocks)
-        pl.when(more)(lambda: forward(c + 3))
         pre_up[...] = dot(rows[...], w_up[...])
         gate = pre_gate[...]
         hidden[...] = (gate * sigma(gate) * pre_up[...]).astype(BF16)
@@ -387,7 +388,7 @@
         scaled_t[...] = turned(scaled[...])
         assemble(c + 2, w_down, hid_blocks, in_blocks)
         extract(c + 2, hidden_t, scaled_t)
-        pl.when(more)(lambda: forward(c + 4))
+        pl.when(more)(lambda: forward(c + 3))
         outs[...] = dot(hidden[...], w_down[...])
         add_part(0, e, (gating * outs[...]).astype(BF16))
         grad_rows = dot(order(e), x_got[1].reshape(all_rows, width))
@@ -402,8 +403,9 @@
                 r_copy(i).start()
             send_back(0)
 
+        pl.when(more)(lambda: forward(c + 4))
+        hidden_grad = dot(scaled[...], w_down[...], ((1,), (1,)))
         pl.when(more)(lambda: forward(c + 5))
-        hidden_grad = dot(scaled[...], w_down[...], ((1,), (1,)))
         gate = pre_gate[...]
         sig = sigma(gate)
         gate_grad = hidden_grad * pre_up[...] * sig * (1.0 + gate * (1.0 - sig))
@@ -446,7 +448,7 @@
                 half_low, pltpu.roll(even, BS, 1), odd
             )
 
-        loop(0, pairs, separate, 4)
+        loop(0, pairs, separate, 8)
         score = jnp.zeros((2 * pairs, LANES), F32)
         for j in range(half):
             part = paired[pl.ds(j, 2 * pairs, stride=half), :]

time: 135 us -> 135 us (level)
  no operation moved by 1% of the time
where the time goes in v2:
time: 135 us; the launch traced here: 134 us
  Pallas kernels  119 us (88%)
  local copies, waits for them, and re-layouts  10.4 us (8%)
  other arithmetic  4.26 us (3%)
    pallas_call x1, Pallas kernels, body(): pl.pallas_call(functools.partial(kernel, (n_dp, n_ex, members, cap)), out...  119 us
    unnamed x13, local copies, waits for them, and re-layouts  8.39 us

profile of v2, /device:TPU:0, one launch (start us, length us, event | category | flops | bytes accessed | tf_op | source)
XLA Modules:
  0.0 134.2 jit_solution(8001278786165829082)
XLA Ops:
  0.7 0.7 copy.25
  1.4 1.5 %fusion.12.pick_ref = s32[768]{0:T(1024)} fusion(s32[768]{0:T(1024)S(1)} %reshape.64, s32[6]{0:T(128)} %constant.104, s32[6]{0:T(128)} %constant.93.clone), kind=kLoop, calls=%fused_computation.33 | loop fusion | flops 12288 | bytes 6192 | tf_op jit(solution)/shard_map/jit(_where)/select_n | solution.py:529
  2.8 0.4 select_reduce_fusion
  3.2 0.8 copy.27
  4.0 0.6 reshape_reshape_squeeze.7.picks_row
  4.6 0.6 fusion.3.place_ref
  5.2 0.7 convert_bitcast_fusion
  5.9 0.6 reshape.71.router
  6.5 0.7 reshape_reshape_squeeze.8.picks_col
  7.3 0.0 copy-start.2
  7.3 118.9 %shard_map.128 = (bf16[256,2048]{1,0:T(8,128)(2,1)}, bf16[256,2048]{1,0:T(8,128)(2,1)}, f32[6,32,4096]{2,1,0:T(8,128)}, f32[6,32,1]{2,1,0:T(8,128)}, f32[2,1,512]{2,1,0:T(1,128)}) custom-call(s32[2304]{0:T(1024)} %fusion.3.place_ref, s32[768]{0:T(1024)} %fusion.12.pick_ref, s32[128,1]{1,0:T(8,128)} %reshape_reshape_squeeze.8.picks_col, ...), custom_call_target="tpu_custom_call" | custom-call | tf_op jit(solution)/shard_map/pallas_call | solution.py:537
  126.1 0.0 copy-start.1
  126.1 1.1 multiply_reduce_fusion
  127.2 0.0 copy-done.2
  127.3 0.6 copy.31
  127.8 1.3 copy.35
  129.1 0.0 copy-start
  129.1 2.5 %copy.39 = bf16[256,2048]{1,0:T(8,128)(2,1)} copy(bf16[256,2048]{1,0:T(8,128)(2,1)} %get-tuple-element.30) | data formatting | bytes 2097152
  131.6 0.0 copy-done.1
  131.6 1.0 copy.40
  132.5 0.0 copy-done
  132.5 1.7 %copy.41 = f32[2,3,32,4096]{3,2,1,0:T(8,128)} copy(f32[2,3,32,4096]{3,2,1,0:T(8,128)S(1)} %bitcast.27) | data formatting | bytes 6291456
  (10 shorter events, 0.1 us)
Async XLA Ops:
  7.3 120.0 %copy-start.2 = (f32[2,3,32]{2,0,1:T(2,128)S(1)}, f32[2,3,32]{2,0,1:T(2,128)}, u32[]{:S(2)}) copy-start(f32[2,3,32]{2,0,1:T(2,128)} %param.15) | copy-start | bytes 2308
  126.1 5.4 %copy-start.1 = (bf16[256,2048]{1,0:T(8,128)(2,1)S(1)}, bf16[256,2048]{1,0:T(8,128)(2,1)}, u32[]{:S(2)}) copy-start(bf16[256,2048]{1,0:T(8,128)(2,1)} %get-tuple-element.31) | copy-start | bytes 3145732
  129.1 3.4 %copy-start = (f32[6,32,4096]{2,1,0:T(8,128)S(1)}, f32[6,32,4096]{2,1,0:T(8,128)}, u32[]{:S(2)}) copy-start(f32[6,32,4096]{2,1,0:T(8,128)} %get-tuple-element.12) | copy-start | bytes 9437188

commit v3 on v2

--- a/solution.py
+++ b/solution.py
@@ -389,20 +389,6 @@
         assemble(c + 2, w_down, hid_blocks, in_blocks)
         extract(c + 2, hidden_t, scaled_t)
         pl.when(more)(lambda: forward(c + 3))
-        outs[...] = dot(hidden[...], w_down[...])
-        add_part(0, e, (gating * outs[...]).astype(BF16))
-        grad_rows = dot(order(e), x_got[1].reshape(all_rows, width))
-        logit = (
-            jnp.sum(grad_rows * outs[...], axis=1, keepdims=True) * gating * (1.0 - gating)
-        )
-        r_send[e] = jnp.sum(rows[...].astype(F32) * logit, axis=0, keepdims=True)
-
-        @pl.when(e == members - 1)
-        def _():
-            for i in range(1, n_dp):
-                r_copy(i).start()
-            send_back(0)
-
         pl.when(more)(lambda: forward(c + 4))
         hidden_grad = dot(scaled[...], w_down[...], ((1,), (1,)))
         pl.when(more)(lambda: forward(c + 5))
@@ -418,6 +404,20 @@
         inner_t[...] = turned(pre_up[...].astype(BF16))
         extract(c + 1, rows_t, inner_t)
         pass_on(c)
+        outs[...] = dot(hidden[...], w_down[...])
+        add_part(0, e, (gating * outs[...]).astype(BF16))
+        grad_rows = dot(order(e), x_got[1].reshape(all_rows, width))
+        logit = (
+            jnp.sum(grad_rows * outs[...], axis=1, keepdims=True) * gating * (1.0 - gating)
+        )
+        r_send[e] = jnp.sum(rows[...].astype(F32) * logit, axis=0, keepdims=True)
+
+        @pl.when(e == members - 1)
+        def _():
+            for i in range(1, n_dp):
+                r_copy(i).start()
+            send_back(0)
+
         part = dot(pre_gate[...].astype(BF16), w_gate[...], ((1,), (1,)))
         part = part + dot(pre_up[...].astype(BF16), w_up[...], ((1,), (1,)))
         add_part(1, e, (part + logit * router[e]).astype(BF16))

time: 135 us -> 140 us (1.037)
  Pallas kernels: 119 us -> 124 us
    pallas_call x1, Pallas kernels: 119 us -> 124 us  [body(): pl.pallas_call(functools.partial(kernel, (n_dp, n_ex, members, cap)), out...]
where the time goes in v3:
time: 140 us; the launch traced here: 139 us
  Pallas kernels  124 us (89%)
  local copies, waits for them, and re-layouts  10.4 us (7%)
  other arithmetic  4.26 us (3%)
    pallas_call x1, Pallas kernels, body(): pl.pallas_call(functools.partial(kernel, (n_dp, n_ex, members, cap)), out...  124 us
    unnamed x13, local copies, waits for them, and re-layouts  8.39 us

profile of v3, /device:TPU:0, one launch (start us, length us, event | category | flops | bytes accessed | tf_op | source)
XLA Modules:
  0.0 139.1 jit_solution(15145730582906556290)
XLA Ops:
  0.7 0.7 copy.25
  1.4 1.5 %fusion.12.pick_ref = s32[768]{0:T(1024)} fusion(s32[768]{0:T(1024)S(1)} %reshape.64, s32[6]{0:T(128)} %constant.104, s32[6]{0:T(128)} %constant.93.clone), kind=kLoop, calls=%fused_computation.33 | loop fusion | flops 12288 | bytes 6192 | tf_op jit(solution)/shard_map/jit(_where)/select_n | solution.py:529
  2.8 0.4 select_reduce_fusion
  3.2 0.8 copy.27
  4.0 0.6 reshape_reshape_squeeze.7.picks_row
  4.6 0.6 fusion.3.place_ref
  5.2 0.7 convert_bitcast_fusion
  5.9 0.6 reshape.71.router
  6.5 0.7 reshape_reshape_squeeze.8.picks_col
  7.3 0.0 copy-start.2
  7.3 123.8 %shard_map.128 = (bf16[256,2048]{1,0:T(8,128)(2,1)}, bf16[256,2048]{1,0:T(8,128)(2,1)}, f32[6,32,4096]{2,1,0:T(8,128)}, f32[6,32,1]{2,1,0:T(8,128)}, f32[2,1,512]{2,1,0:T(1,128)}) custom-call(s32[2304]{0:T(1024)} %fusion.3.place_ref, s32[768]{0:T(1024)} %fusion.12.pick_ref, s32[128,1]{1,0:T(8,128)} %reshape_reshape_squeeze.8.picks_col, ...), custom_call_target="tpu_custom_call" | custom-call | tf_op jit(solution)/shard_map/pallas_call | solution.py:537
  131.1 0.0 copy-start.1
  131.1 1.1 multiply_reduce_fusion
  132.2 0.0 copy-done.2
  132.2 0.6 copy.31
  132.8 1.3 copy.35
  134.0 0.0 copy-start
  134.0 2.5 %copy.39 = bf16[256,2048]{1,0:T(8,128)(2,1)} copy(bf16[256,2048]{1,0:T(8,128)(2,1)} %get-tuple-element.30) | data formatting | bytes 2097152
  136.5 0.0 copy-done.1
  136.5 1.0 copy.40
  137.5 0.0 copy-done
  137.5 1.7 %copy.41 = f32[2,3,32,4096]{3,2,1,0:T(8,128)} copy(f32[2,3,32,4096]{3,2,1,0:T(8,128)S(1)} %bitcast.27) | data formatting | bytes 6291456
  (10 shorter events, 0.1 us)
Async XLA Ops:
  7.3 124.9 %copy-start.2 = (f32[2,3,32]{2,0,1:T(2,128)S(1)}, f32[2,3,32]{2,0,1:T(2,128)}, u32[]{:S(2)}) copy-start(f32[2,3,32]{2,0,1:T(2,128)} %param.15) | copy-start | bytes 2308
  131.1 5.4 %copy-start.1 = (bf16[256,2048]{1,0:T(8,128)(2,1)S(1)}, bf16[256,2048]{1,0:T(8,128)(2,1)}, u32[]{:S(2)}) copy-start(bf16[256,2048]{1,0:T(8,128)(2,1)} %get-tuple-element.31) | copy-start | bytes 3145732
  134.0 3.4 %copy-start = (f32[6,32,4096]{2,1,0:T(8,128)S(1)}, f32[6,32,4096]{2,1,0:T(8,128)}, u32[]{:S(2)}) copy-start(f32[6,32,4096]{2,1,0:T(8,128)} %get-tuple-element.12) | copy-start | bytes 9437188
